TPU v7x, 32 devices: a whole 2x2x4 slice. The times are simulated.
32 devices in a mesh: fsdp: 4 (over y, x), ctx: 8 (over z, core).
Axes of the slice: x: 2, y: 2, z: 4, core: 2. Of those that a mesh axis runs over, the one named last changes fastest.
Arguments:
- inputs: bfloat16 [4, 1024, 2048], P('fsdp', 'ctx'), may hold values from -6 to 6
- queries: bfloat16 [4, 1024, 3072], P('fsdp', 'ctx'), may hold values from -210 to 210
- kv_down: bfloat16 [2048, 576], replicated, may hold values from -0.125 to 0.125
- latent_gain: bfloat16 [512], replicated, may hold values from 0.25 to 1.75
- kv_up: bfloat16 [512, 4096], replicated, may hold values from -0.25 to 0.25
- out_proj: bfloat16 [2048, 2048], replicated, may hold values from -0.125 to 0.125
- post_gain: bfloat16 [2048], replicated, may hold values from 0.25 to 1.75
- expert_ids: int32 [4, 1024, 6], P('fsdp', 'ctx'), may hold values from 0 to 15, all different within a row; in each aligned block of 128 rows (0 to 127, 128 to 255, ..., all dimensions but the last counted through in order) at most 96 rows name the same one
- gates: float32 [4, 1024, 6], P('fsdp', 'ctx'), may hold values from 0.1 to 1
- gate_up: bfloat16 [16, 2048, 1536], P('ctx', 'fsdp'), may hold values from -0.125 to 0.125
- down_proj: bfloat16 [16, 2048, 768], P('ctx', 'fsdp'), may hold values from -0.21875 to 0.21875
Outputs:
- attn_out: bfloat16 [4, 1024, 2048], P('fsdp', 'ctx')
- moe_out: bfloat16 [4, 1024, 2048], P('fsdp', 'ctx')
Inputs may be any that keep to these rules, and one draw needn't show every extreme that they name: `expert_ids`: within the 128 consecutive positions of a sequence on one index of ctx, no expert is chosen by more than 96 picks, a bound that some block reaches. The 6 experts of a token differ.
All inputs are finite; a program needn't handle non-finite values.
Results may differ from a plain program's by a relative error of at most 0.02.
The roundings to bfloat16 on the way count: a program that leaves them out, or rounds other values in their place, can miss the bound.
Values may be sent and summed in bfloat16 or wider, within the bound.
No kernel may reach another device: no remote copies, remote signals or barrier semaphores. Data moves between devices by JAX's collectives and lax.ppermute only.
A program may use at most 192 MiB of HBM per device.

v0:
```python
import math
import jax
import jax.numpy as jnp
from jax import lax
from jax.sharding import PartitionSpec as P

HEADS = 16
NOPE = 128
ROPE = 64
VDIM = 128
EPSILON = 1e-06
NEG_LARGE = -1e30


def normalize(values, gain):
    mean_sq = jnp.mean(values * values, axis=-1, keepdims=True)
    return values * lax.rsqrt(mean_sq + EPSILON) * gain.astype(jnp.float32)


def rotate(values, angles):
    half = values.shape[-1] // 2
    first = values[..., :half]
    second = values[..., half:]
    cosine = jnp.cos(angles)
    sine = jnp.sin(angles)
    return jnp.concatenate(
        [first * cosine - second * sine, second * cosine + first * sine], axis=-1
    )


def angles_of(positions, width):
    half = width // 2
    freqs = jnp.exp(-(2.0 * jnp.arange(half, dtype=jnp.float32) / width) * math.log(10000.0))
    return positions.astype(jnp.float32)[:, None] * freqs[None, :]


def attend(state, query_rows, row_pos, piece, start, latent_width):

    def update(inner):
        peak_old, total_old, acc_old = inner
        scores = jnp.dot(query_rows, jnp.transpose(piece), preferred_element_type=jnp.float32)
        key_pos = jnp.arange(piece.shape[0], dtype=jnp.int32)
        allowed = key_pos[None, :] <= row_pos[:, None]
        scores = jnp.where(allowed, scores, NEG_LARGE)
        peak_new = jnp.maximum(peak_old, jnp.max(scores, axis=1))
        expo = jnp.where(allowed, jnp.exp(scores - peak_new[:, None]), 0.0)
        total_new = jnp.sum(expo, axis=1)
        values = piece[:, :latent_width]
        acc_new = jnp.dot(expo.astype(jnp.bfloat16), values, preferred_element_type=jnp.float32)
        return (peak_new, total_new, acc_new)

    def keep(inner):
        return inner

    return lax.cond(start <= jnp.max(row_pos), update, keep, state)


def per_device(
    inputs,
    queries,
    kv_down,
    latent_gain,
    kv_up,
    out_proj,
    post_gain,
    expert_ids,
    gates,
    gate_up,
    down_proj,
):
    tokens = inputs[0]
    rows = tokens.shape[0]
    width_model = tokens.shape[1]
    ctx_size = lax.axis_size("ctx")
    rank = lax.axis_index("ctx")
    positions = rank * rows + jnp.arange(rows, dtype=jnp.int32)
    angles = angles_of(positions, ROPE)
    latent_width = latent_gain.shape[0]
    compressed = jnp.dot(tokens, kv_down, preferred_element_type=jnp.float32)
    latent = normalize(compressed[:, :latent_width], latent_gain)
    key_rope = rotate(compressed[:, latent_width:], angles)
    cache = jnp.concatenate([latent, key_rope], axis=1).astype(jnp.bfloat16)
    up_heads = kv_up.reshape(latent_width, HEADS, NOPE + VDIM)
    scale = (NOPE + ROPE) ** (-0.5)
    half = rows // 2
    query_heads = queries[0].reshape(rows, HEADS, NOPE + ROPE)
    lower_query = query_heads[:half]
    upper_query = query_heads[half:]
    lower_pos = positions[:half]
    upper_pos = positions[half:]

    def pack_rows(query_part, query_pos):
        part_angles = angles_of(query_pos, ROPE)
        absorbed = jnp.einsum(
            "thn,lhn->thl",
            query_part[:, :, :NOPE],
            up_heads[:, :, :NOPE],
            preferred_element_type=jnp.float32,
        )
        query_rope = rotate(query_part[:, :, NOPE:].astype(jnp.float32), part_angles[:, None, :])
        packed_part = (jnp.concatenate([absorbed, query_rope], axis=2) * scale).astype(jnp.bfloat16)
        return packed_part.reshape(half * HEADS, packed_part.shape[2])

    lower_rows = pack_rows(lower_query, lower_pos)
    upper_rows = pack_rows(upper_query, upper_pos)
    lower_row_pos = jnp.repeat(lower_pos, HEADS)
    upper_row_pos = jnp.repeat(upper_pos, HEADS)

    def start_state():
        return (
            jnp.full((half * HEADS,), NEG_LARGE, jnp.float32),
            jnp.zeros((half * HEADS,), jnp.float32),
            jnp.zeros((half * HEADS, latent_width), jnp.float32),
        )

    piece = lax.all_gather(cache, "ctx", axis=0, tiled=True)
    start = jnp.int32(0)
    first = attend(start_state(), lower_rows, lower_row_pos, piece, start, latent_width)
    second = attend(start_state(), upper_rows, upper_row_pos, piece, start, latent_width)

    def head_rows(state):
        context_part = (
            (state[2] / state[1][:, None]).astype(jnp.bfloat16).reshape(half, HEADS, latent_width)
        )
        heads_part = jnp.einsum(
            "thl,lhv->thv", context_part, up_heads[:, :, NOPE:], preferred_element_type=jnp.float32
        )
        return heads_part.astype(jnp.bfloat16).reshape(half, HEADS * VDIM)

    lower_heads = head_rows(first)
    upper_heads = head_rows(second)
    heads = jnp.concatenate([lower_heads, upper_heads], axis=0)
    attn = jnp.dot(heads, out_proj, preferred_element_type=jnp.float32)
    attn_out = attn.astype(jnp.bfloat16)
    routed_in = normalize(tokens.astype(jnp.float32) + attn, post_gain).astype(jnp.bfloat16)
    local_experts = gate_up.shape[0]
    experts = local_experts * ctx_size
    top_count = expert_ids.shape[2]
    capacity = 2 * rows * top_count // experts
    picks = expert_ids[0].reshape(rows * top_count)
    onehot = (picks[:, None] == jnp.arange(experts, dtype=jnp.int32)[None, :]).astype(jnp.int32)
    before = jnp.cumsum(onehot, axis=0) - onehot
    slot = jnp.sum(before * onehot, axis=1)
    target = picks * capacity + slot
    owner = jnp.arange(rows * top_count, dtype=jnp.int32) // top_count
    outgoing = (
        jnp.zeros((experts * capacity, width_model), jnp.bfloat16).at[target].set(routed_in[owner])
    )
    arrived = lax.all_to_all(
        outgoing.reshape(experts, capacity, width_model),
        "ctx",
        split_axis=0,
        concat_axis=1,
        tiled=True,
    )
    hidden_width = down_proj.shape[2]
    full_gate_up, full_down = (
        lax.all_gather(gate_up, "fsdp", axis=1, tiled=True),
        lax.all_gather(down_proj, "fsdp", axis=1, tiled=True),
    )
    joint = jnp.einsum("erd,edf->erf", arrived, full_gate_up, preferred_element_type=jnp.float32)
    hidden = (jax.nn.silu(joint[..., :hidden_width]) * joint[..., hidden_width:]).astype(
        jnp.bfloat16
    )
    results = jnp.einsum("erf,edf->erd", hidden, full_down, preferred_element_type=jnp.float32)
    returned = lax.all_to_all(
        results.astype(jnp.bfloat16), "ctx", split_axis=1, concat_axis=0, tiled=True
    )
    picked = returned.reshape(experts * capacity, width_model)[target]
    weighted = picked.astype(jnp.float32) * gates[0].reshape(rows * top_count)[:, None]
    moe = jnp.sum(weighted.reshape(rows, top_count, width_model), axis=1).astype(jnp.bfloat16)
    return (attn_out[None], moe[None])


def solution(mesh):
    in_specs = (
        P("fsdp", "ctx", None),
        P("fsdp", "ctx", None),
        P(),
        P(),
        P(),
        P(),
        P(),
        P("fsdp", "ctx", None),
        P("fsdp", "ctx", None),
        P("ctx", "fsdp", None),
        P("ctx", "fsdp", None),
    )
    out_specs = (P("fsdp", "ctx", None), P("fsdp", "ctx", None))
    return jax.shard_map(
        per_device, mesh=mesh, in_specs=in_specs, out_specs=out_specs, check_vma=False
    )
```

profile of v0, /device:TPU:0, one launch (start us, length us, event | category | flops | bytes accessed | tf_op | source)
XLA Modules:
  0.0 487.7 jit_solution(18436922709212303032)
XLA Ops:
  15.0 6.5 %copy.39 = bf16[512,4096]{0,1:T(8,128)(2,1)} copy(bf16[512,4096]{1,0:T(8,128)(2,1)} %param.19) | data formatting | bytes 8388608 | tf_op args[4]
  29.9 2.6 copy.48
  41.7 13.9 %conditional.2 = (f32[1024]{0:T(1024)S(1)}, f32[1024,512]{1,0:T(8,128)S(1)}) conditional(s32[]{:T(128)} %convert_element_type.106, () %tuple.24, (s32[64,16]{1,0:T(8,128)S(1)}, bf16[1024,576]{1,0:T(8,128)(2,1)}, bf16[1024,576]{0,1:T(8,128)(2,1)}) %tuple.25), branch_computations={%region_2.0_spmd, %region_3.6_spmd} | conditional | flops 2295331840 | bytes 41988168 | solution.py:55
  42.0 5.7 %fusion.1 = (f32[1024]{0:T(1024)S(1)}, f32[1024,1024]{0,1:T(8,128)}) fusion(s32[1024]{0:T(1024)S(1)} %le.3, bf16[1024,576]{1,0:T(8,128)(2,1)} %get-tuple-element.13, bf16[1024,576]{0,1:T(8,128)(2,1)} %get-tuple-element.42), kind=kOutput, calls=%fused_computation.6 | convolution fusion | flops 1211104256 | bytes 6561792 | tf_op jit(solution)/shard_map/cond/branch_1_fun/dot_general | solution.py:41
  49.1 4.7 fusion.4
  55.8 2.5 fusion.54
  59.1 13.2 %conditional.3 = (f32[1024]{0:T(1024)}, f32[1024,512]{1,0:T(8,128)S(1)}) conditional(s32[]{:T(128)} %convert_element_type.115, () %tuple.26, (s32[64,16]{1,0:T(8,128)}, bf16[1024,576]{1,0:T(8,128)(2,1)}, bf16[1024,576]{0,1:T(8,128)(2,1)S(1)}) %tuple.61), branch_computations={%region_7.8_spmd, %region_8.11_spmd} | conditional | flops 2295331840 | bytes 37269548 | solution.py:55
  59.9 5.2 %fusion.14 = (f32[1024]{0:T(1024)S(1)}, f32[1024,1024]{0,1:T(8,128)}) fusion(s32[1024]{0:T(1024)S(1)} %le.22, bf16[1024,576]{1,0:T(8,128)(2,1)} %get-tuple-element.16, bf16[1024,576]{0,1:T(8,128)(2,1)S(1)} %get-tuple-element.45), kind=kOutput, calls=%fused_computation.21 | convolution fusion | flops 1211104256 | bytes 6561792 | tf_op jit(solution)/shard_map/cond/branch_1_fun/dot_general | solution.py:41
  66.6 3.9 fusion.17
  73.3 2.4 fusion.57
  75.8 4.8 multiply_reduce_fusion.1
  81.6 24.7 %scatter_custom_fusion = bf16[1536,2048]{1,0:T(8,128)(2,1)} fusion(s32[768]{0:T(1024)S(1)} %copy-done.9, bf16[128,2048]{1,0:T(8,128)(2,1)S(1)} %get-tuple-element.50, s32[1024]{0:T(1024)} %pad_clamp_fusion.1, bf16[]{:T(256)} %constant.32.clone.1), kind=kCustom, calls=%fused_computation.37 | custom fusion | bytes 6291968 | tf_op jit(solution)/shard_map/scatter | solution.py:147
  106.4 6.5 %all-to-all-start = ((bf16[16,96,2048]{2,1,0:T(8,128)(2,1)}), bf16[16,96,2048]{2,1,0:T(8,128)(2,1)}, u32[]{:S(2)}, u32[]{:S(2)}) async-start(bf16[16,96,2048]{2,1,0:T(8,128)(2,1)} %bitcast.75), calls=%async_computation | async-start | bytes 12582912 | tf_op jit(solution)/shard_map/all_to_all | solution.py:149
  113.6 138.3 %all-to-all-done = bf16[16,96,2048]{2,1,0:T(8,128)(2,1)} async-done(((bf16[16,96,2048]{2,1,0:T(8,128)(2,1)}), bf16[16,96,2048]{2,1,0:T(8,128)(2,1)}, u32[]{:S(2)}, u32[]{:S(2)}) %all-to-all-start) | async-done | bytes 6291488 | tf_op jit(solution)/shard_map/all_to_all | solution.py:149
  251.9 6.5 %copy.56 = bf16[2,8,96,2048]{3,2,1,0:T(8,128)(2,1)} copy(bf16[2,8,96,2048]{3,2,0,1:T(8,128)(2,1)} %bitcast.18) | data formatting | bytes 12582912 | tf_op jit(solution)/shard_map/all_to_all | solution.py:149
  258.5 17.0 %fusion.88 = f32[2,768,1536]{2,1,0:T(8,128)} fusion(bf16[2,768,2048]{2,1,0:T(8,128)(2,1)} %bitcast.82, bf16[2,2048,1536]{2,1,0:T(8,128)(2,1)} %all-gather.6.cloned.1.call-done), kind=kOutput, calls=%fused_computation.133 | convolution fusion | flops 9663676416 | bytes 28311552 | tf_op jit(solution)/shard_map/erd,edf->erf/dot_general | solution.py:161
  275.5 9.6 %convolution_convert_fusion = bf16[2,768,2048]{2,1,0:T(8,128)(2,1)S(1)} fusion(bf16[2,2048,768]{2,1,0:T(8,128)(2,1)} %all-gather.8.cloned.1.call-done, f32[2,768,1536]{2,1,0:T(8,128)} %fusion.88), kind=kOutput, calls=%fused_computation.36 | convolution fusion | flops 4842061824 | bytes 22020096 | tf_op jit(solution)/shard_map/erf,edf->erd/dot_general | solution.py:165
  285.0 18.8 %copy.57 = bf16[2,768,2048]{2,0,1:T(2,128)(2,1)} copy(bf16[2,768,2048]{2,1,0:T(8,128)(2,1)S(1)} %convolution_convert_fusion) | data formatting | bytes 12582912 | tf_op jit(solution)/shard_map/convert_element_type | solution.py:167
  303.8 5.0 %all-to-all-start.1 = ((bf16[2,768,2048]{2,0,1:T(2,128)(2,1)}), bf16[2,768,2048]{2,0,1:T(2,128)(2,1)}, u32[]{:S(2)}, u32[]{:S(2)}) async-start(bf16[2,768,2048]{2,0,1:T(2,128)(2,1)} %copy.57), calls=%async_computation.1 | async-start | bytes 12582912 | tf_op jit(solution)/shard_map/all_to_all | solution.py:166
  309.0 138.8 %all-to-all-done.1 = bf16[2,768,2048]{2,0,1:T(2,128)(2,1)} async-done(((bf16[2,768,2048]{2,0,1:T(2,128)(2,1)}), bf16[2,768,2048]{2,0,1:T(2,128)(2,1)}, u32[]{:S(2)}, u32[]{:S(2)}) %all-to-all-start.1) | async-done | bytes 6291488 | tf_op jit(solution)/shard_map/all_to_all | solution.py:166
  447.8 8.3 %copy.58 = bf16[2,8,96,2048]{3,2,0,1:T(8,128)(2,1)} copy(bf16[2,8,96,2048]{3,0,2,1:T(2,128)(2,1)} %bitcast.20) | data formatting | bytes 12582912 | tf_op jit(solution)/shard_map/all_to_all | solution.py:166
  456.1 10.7 %gather_fusion = bf16[768,2048]{1,0:T(8,128)(2,1)} fusion(bf16[1536,2048]{1,0:T(8,128)(2,1)} %bitcast.74, s32[1024]{0:T(1024)S(1)} %pad_clamp_fusion), kind=kCustom, calls=%fused_computation.1 | custom fusion | bytes 6294528 | tf_op jit(solution)/shard_map/gather | solution.py:169
  466.8 6.6 %reshape.286 = f32[128,6,2048]{2,1,0:T(8,128)} reshape(bf16[768,2048]{1,0:T(8,128)(2,1)} %gather_fusion) | data formatting | bytes 9437184 | tf_op jit(solution)/shard_map/convert_element_type | solution.py:170
  473.4 7.5 %multiply_reduce_fusion = bf16[128,2048]{1,0:T(8,128)(2,1)} fusion(f32[128,6,2048]{2,1,0:T(8,128)} %reshape.286, f32[128,6]{1,0:T(8,128)S(1)} %bitcast.92), kind=kLoop, calls=%fused_computation.33 | loop fusion | flops 2883584 | bytes 6818816 | tf_op jit(solution)/shard_map/reduce_sum | solution.py:171
  (95 shorter events, 35.2 us)
Async XLA Ops:
  7.2 1.7 copy-start
  7.2 6.0 %copy-start.10 = (s32[1,128,6]{1,0,2:T(1,128)S(1)}, s32[1,128,6]{1,0,2:T(1,128)}, u32[]{:S(2)}) copy-start(s32[1,128,6]{1,0,2:T(1,128)} %param.22) | copy-start | bytes 9220
  7.2 6.4 %copy-start.8 = (bf16[1,128,3072]{2,1,0:T(8,128)(2,1)S(1)}, bf16[1,128,3072]{2,1,0:T(8,128)(2,1)}, u32[]{:S(2)}) copy-start(bf16[1,128,3072]{2,1,0:T(8,128)(2,1)} %param.16) | copy-start | bytes 2359300
  7.2 34.5 %all-gather.4.cloned.1.call-start = ((), (), s32[]{:S(2)}) async-start(), calls=%async_computation.2 | async-start | bytes 1327104 | tf_op jit(solution)/shard_map/all_gather | solution.py:116
  12.4 246.1 %all-gather.6.cloned.1.call-start = ((), (), s32[]{:S(2)}) async-start(), calls=%async_computation.3 | async-start | bytes 15728640 | tf_op jit(solution)/shard_map/all_gather | solution.py:158
  27.9 6.0 %copy-start.11 = (bf16[2048]{0:T(1024)(128)(2,1)S(1)}, bf16[2048]{0:T(1024)(128)(2,1)}, u32[]{:S(2)}) copy-start(bf16[2048]{0:T(1024)(128)(2,1)} %param.21) | copy-start | bytes 12292
  38.1 2.1 copy-start.2
  42.0 5.7 %copy-start.5 = (bf16[1024,576]{0,1:T(8,128)(2,1)S(1)}, bf16[1024,576]{0,1:T(8,128)(2,1)}, u32[]{:S(2)}) copy-start(bf16[1024,576]{0,1:T(8,128)(2,1)} %get-tuple-element.42) | copy-start | bytes 3538948 | tf_op jit(solution)/shard_map/cond
  49.1 5.3 %copy-start.6 = (f32[1024,1024]{0,1:T(8,128)S(1)}, f32[1024,1024]{0,1:T(8,128)}, u32[]{:S(2)}) copy-start(f32[1024,1024]{0,1:T(8,128)} %get-tuple-element.47) | copy-start | bytes 12582916 | tf_op jit(solution)/shard_map/cond
  55.6 3.5 copy-start.4
  66.6 4.0 copy-start.7
  72.3 3.5 copy-start.3
  75.8 5.9 %copy-start.9 = (s32[768]{0:T(1024)S(1)}, s32[768]{0:T(1024)}, u32[]{:S(2)}) copy-start(s32[768]{0:T(1024)} %fusion.82) | copy-start | bytes 9220
  106.4 145.6 %all-to-all-start = ((bf16[16,96,2048]{2,1,0:T(8,128)(2,1)}), bf16[16,96,2048]{2,1,0:T(8,128)(2,1)}, u32[]{:S(2)}, u32[]{:S(2)}) async-start(bf16[16,96,2048]{2,1,0:T(8,128)(2,1)} %bitcast.75), calls=%async_computation | async-start | bytes 12582912 | tf_op jit(solution)/shard_map/all_to_all | solution.py:149
  112.9 162.6 %all-gather.8.cloned.1.call-start = ((), (), s32[]{:S(2)}) async-start(), calls=%async_computation.4 | async-start | bytes 7864320 | tf_op jit(solution)/shard_map/all_gather | solution.py:159
  303.8 5.1 %copy-start.12 = (f32[1,128,6]{1,0,2:T(1,128)S(1)}, f32[1,128,6]{1,0,2:T(1,128)}, u32[]{:S(2)}) copy-start(f32[1,128,6]{1,0,2:T(1,128)} %param.23) | copy-start | bytes 9220
  303.8 144.0 %all-to-all-start.1 = ((bf16[2,768,2048]{2,0,1:T(2,128)(2,1)}), bf16[2,768,2048]{2,0,1:T(2,128)(2,1)}, u32[]{:S(2)}, u32[]{:S(2)}) async-start(bf16[2,768,2048]{2,0,1:T(2,128)(2,1)} %copy.57), calls=%async_computation.1 | async-start | bytes 12582912 | tf_op jit(solution)/shard_map/all_to_all | solution.py:166
  473.4 7.5 %copy-start.1 = (bf16[2048,576]{0,1:T(8,128)(2,1)S(1)}, bf16[2048,576]{0,1:T(8,128)(2,1)}, u32[]{:S(2)}) copy-start(bf16[2048,576]{0,1:T(8,128)(2,1)} %param.17) | copy-start | bytes 7077892
Sparse Core Ops, SparseCore 0:
  12.5 27.4 all-gather.3
  41.9 121.3 all-gather.5
  165.1 70.1 all-gather.7
where the time goes:
time: 495 us; the launch traced here: 488 us
  waiting for transfers between devices  279 us (56%)
  local copies, waits for them, and re-layouts  97.1 us (20%)
  matrix products  61.8 us (12%)
  other arithmetic  22.9 us (5%)
  between operations  15.5 us (3%)
  starting transfers between devices  11.7 us (2%)
    all_to_all x1, waiting for transfers between devices, per_device(): lax.all_to_all(results.astype(jnp.bfloat16), 'ctx', split_axis=1, concat_...  139 us
    all_to_all x1, waiting for transfers between devices, per_device(): lax.all_to_all(outgoing.reshape(experts, capacity, width_model), 'ctx', s...  138 us
    scatter x1, local copies, waits for them, and re-layouts, per_device(): jnp.zeros((experts * capacity, width_model), jnp.bfloat16).at[target]  24.7 us
    convert_element_type x1, local copies, waits for them, and re-layouts, per_device(): results.astype(jnp.bfloat16)  18.8 us
    dot_general x1, matrix products, per_device(): jnp.einsum('erd,edf->erf', arrived, full_gate_up, preferred_element_type=...  17 us
    dot_general x2, matrix products, update(): jnp.dot(query_rows, jnp.transpose(piece), preferred_element_type=jnp.floa...  10.9 us
    gather x1, local copies, waits for them, and re-layouts, per_device(): picked = returned.reshape(experts * capacity, width_model)[target]  10.7 us
  transfers between devices with their start and end apart: 5, of which 2 were waited for; matrix products, arithmetic and copies ran while one was open for 23% of the time, Pallas kernels for 0%

commit v1 on v0

--- a/solution.py
+++ b/solution.py
@@ -10,6 +10,31 @@
 VDIM = 128
 EPSILON = 1e-06
 NEG_LARGE = -1e30
+
+
+def in_blocks(shard, dim, size):
+    before, after = (shard.shape[:dim], shard.shape[dim + 1 :])
+    return jnp.moveaxis(shard.reshape(*before, size, -1, *after), dim, 0)
+
+
+def laid_out(tiles, dim):
+    tiles = jnp.moveaxis(tiles, 0, dim)
+    lengths = tiles.shape
+    return tiles.reshape(*lengths[:dim], lengths[dim] * lengths[dim + 1], *lengths[dim + 2 :])
+
+
+def rotated_exchange(x, axis, split_dim, concat_dim):
+    devices, index = (lax.axis_size(axis), lax.axis_index(axis))
+    pieces = in_blocks(x, split_dim, devices)
+    out = pieces
+    for step in range(1, devices):
+        target, source = ((index + step) % devices, (index - step) % devices)
+        sent = lax.dynamic_index_in_dim(pieces, target, 0)
+        partner_block = lax.ppermute(
+            sent, axis, [(i, (i + step) % devices) for i in range(devices)]
+        )
+        out = lax.dynamic_update_slice_in_dim(out, partner_block, source, axis=0)
+    return laid_out(out, concat_dim)
 
 
 def normalize(values, gain):
@@ -163,9 +188,7 @@
         jnp.bfloat16
     )
     results = jnp.einsum("erf,edf->erd", hidden, full_down, preferred_element_type=jnp.float32)
-    returned = lax.all_to_all(
-        results.astype(jnp.bfloat16), "ctx", split_axis=1, concat_axis=0, tiled=True
-    )
+    returned = rotated_exchange(results.astype(jnp.bfloat16), "ctx", 1, 0)
     picked = returned.reshape(experts * capacity, width_model)[target]
     weighted = picked.astype(jnp.float32) * gates[0].reshape(rows * top_count)[:, None]
     moe = jnp.sum(weighted.reshape(rows, top_count, width_model), axis=1).astype(jnp.bfloat16)

time: 495 us -> 473 us (0.956)
  the two profiles are of different devices: /device:TPU:0 before, /device:TPU:9 now
where the time goes in v1:
time: 473 us; the launch traced here: 466 us
  waiting for transfers between devices  259 us (55%)
  local copies, waits for them, and re-layouts  91.2 us (19%)
  matrix products  62.2 us (13%)
  other arithmetic  22.9 us (5%)
  between operations  15.8 us (3%)
  starting transfers between devices  14 us (3%)
    all_to_all x1, waiting for transfers between devices, per_device(): lax.all_to_all(outgoing.reshape(experts, capacity, width_model), 'ctx', s...  135 us
    ppermute x7, waiting for transfers between devices, rotated_exchange(): lax.ppermute(sent, axis, [(i, (i + step) % devices) for i in range(device...  123 us
    scatter x1, local copies, waits for them, and re-layouts, per_device(): jnp.zeros((experts * capacity, width_model), jnp.bfloat16).at[target]  24.7 us
    dynamic_update_slice x8, local copies, waits for them, and re-layouts, rotated_exchange(): out = lax.dynamic_update_slice_in_dim(out, partner_block, source, axis=0)  17.9 us
    dot_general x1, matrix products, per_device(): jnp.einsum('erd,edf->erf', arrived, full_gate_up, preferred_element_type=...  17 us
    dot_general x2, matrix products, update(): jnp.dot(query_rows, jnp.transpose(piece), preferred_element_type=jnp.floa...  11.3 us
    gather x1, local copies, waits for them, and re-layouts, per_device(): picked = returned.reshape(experts * capacity, width_model)[target]  10.7 us
    unnamed x24, local copies, waits for them, and re-layouts  9.73 us
  transfers between devices with their start and end apart: 11, of which 6 were waited for; matrix products, arithmetic and copies ran while one was open for 27% of the time, Pallas kernels for 0%

profile of v1, /device:TPU:9, one launch (start us, length us, event | category | flops | bytes accessed | tf_op | source)
XLA Modules:
  0.0 465.8 jit_solution(13681226586566614193)
XLA Ops:
  15.0 6.5 %copy.19 = bf16[512,4096]{0,1:T(8,128)(2,1)} copy(bf16[512,4096]{1,0:T(8,128)(2,1)} %param.19) | data formatting | bytes 8388608 | tf_op args[4]
  30.1 2.6 copy.28
  41.8 14.2 %conditional.2 = (f32[1024]{0:T(1024)S(1)}, f32[1024,512]{1,0:T(8,128)S(1)}) conditional(s32[]{:T(128)} %convert_element_type.106, () %tuple.24, (s32[64,16]{1,0:T(8,128)S(1)}, bf16[1024,576]{1,0:T(8,128)(2,1)}, bf16[1024,576]{0,1:T(8,128)(2,1)}) %tuple.25), branch_computations={%region_2.0_spmd, %region_3.6_spmd} | conditional | flops 2295331840 | bytes 41988168 | solution.py:80
  42.0 6.1 %fusion.1 = (f32[1024]{0:T(1024)S(1)}, f32[1024,1024]{0,1:T(8,128)}) fusion(s32[1024]{0:T(1024)S(1)} %le.3, bf16[1024,576]{1,0:T(8,128)(2,1)} %get-tuple-element.13, bf16[1024,576]{0,1:T(8,128)(2,1)} %get-tuple-element.36), kind=kOutput, calls=%fused_computation.6 | convolution fusion | flops 1211104256 | bytes 6561792 | tf_op jit(solution)/shard_map/cond/branch_1_fun/dot_general | solution.py:66
  49.6 4.7 %fusion.4 = f32[1024,512]{1,0:T(8,128)S(1)} fusion(f32[1024,1024]{0,1:T(8,128)} %get-tuple-element.41, f32[1024]{0:T(1024)S(1)} %broadcast_maximum_fusion, s32[1024]{0:T(1024)S(1)} %le.3, bf16[1024,576]{1,0:T(8,128)(2,1)} %copy.23), kind=kOutput, calls=%fused_computation.9 | convolution fusion | flops 1078984704 | bytes 7348224 | tf_op jit(solution)/shard_map/cond/branch_1_fun/dot_general | solution.py:74
  56.2 2.5 fusion.54
  59.5 13.2 %conditional.3 = (f32[1024]{0:T(1024)}, f32[1024,512]{1,0:T(8,128)S(1)}) conditional(s32[]{:T(128)} %convert_element_type.115, () %tuple.26, (s32[64,16]{1,0:T(8,128)}, bf16[1024,576]{1,0:T(8,128)(2,1)}, bf16[1024,576]{0,1:T(8,128)(2,1)S(1)}) %tuple.66), branch_computations={%region_7.8_spmd, %region_8.11_spmd} | conditional | flops 2295331840 | bytes 37269548 | solution.py:80
  60.4 5.2 %fusion.14 = (f32[1024]{0:T(1024)S(1)}, f32[1024,1024]{0,1:T(8,128)}) fusion(s32[1024]{0:T(1024)S(1)} %le.22, bf16[1024,576]{1,0:T(8,128)(2,1)} %get-tuple-element.16, bf16[1024,576]{0,1:T(8,128)(2,1)S(1)} %get-tuple-element.39), kind=kOutput, calls=%fused_computation.21 | convolution fusion | flops 1211104256 | bytes 6561792 | tf_op jit(solution)/shard_map/cond/branch_1_fun/dot_general | solution.py:66
  67.0 3.9 fusion.17
  76.2 4.8 %multiply_reduce_fusion.1 = (f32[128]{0:T(128)S(1)}, f32[128,2048]{1,0:T(8,128)S(1)}) fusion(bf16[1,128,2048]{2,1,0:T(8,128)(2,1)S(1)} %copy-done.4, bf16[2048,2048]{1,0:T(8,128)(2,1)} %param.20, bf16[64,2048]{1,0:T(8,128)(2,1)S(1)} %bitcast.104, bf16[64,2048]{1,0:T(8,128)(2,1)S(1)} %bitcast.103), kind=kOutput, calls=%fused_computation.64 | convolution fusion | flops 1075838848 | bytes 10486272 | tf_op jit(solution)/shard_map/dot_general | solution.py:158
  82.1 24.7 %scatter_custom_fusion = bf16[1536,2048]{1,0:T(8,128)(2,1)} fusion(s32[768]{0:T(1024)S(1)} %copy-done.10, bf16[128,2048]{1,0:T(8,128)(2,1)S(1)} %get-tuple-element.51, s32[1024]{0:T(1024)} %pad_clamp_fusion.1, bf16[]{:T(256)} %constant.157.clone.1), kind=kCustom, calls=%fused_computation.37 | custom fusion | bytes 6291968 | tf_op jit(solution)/shard_map/scatter | solution.py:172
  106.8 5.5 %all-to-all-start = ((bf16[16,96,2048]{2,1,0:T(8,128)(2,1)}), bf16[16,96,2048]{2,1,0:T(8,128)(2,1)}, u32[]{:S(2)}, u32[]{:S(2)}) async-start(bf16[16,96,2048]{2,1,0:T(8,128)(2,1)} %bitcast.89), calls=%async_computation | async-start | bytes 12582912 | tf_op jit(solution)/shard_map/all_to_all | solution.py:174
  113.1 134.6 %all-to-all-done = bf16[16,96,2048]{2,1,0:T(8,128)(2,1)} async-done(((bf16[16,96,2048]{2,1,0:T(8,128)(2,1)}), bf16[16,96,2048]{2,1,0:T(8,128)(2,1)}, u32[]{:S(2)}, u32[]{:S(2)}) %all-to-all-start) | async-done | bytes 6291488 | tf_op jit(solution)/shard_map/all_to_all | solution.py:174
  247.7 6.5 %copy.36 = bf16[2,8,96,2048]{3,2,1,0:T(8,128)(2,1)} copy(bf16[2,8,96,2048]{3,2,0,1:T(8,128)(2,1)} %bitcast.18) | data formatting | bytes 12582912 | tf_op jit(solution)/shard_map/all_to_all | solution.py:174
  254.2 17.0 %fusion.88 = f32[2,768,1536]{2,1,0:T(8,128)} fusion(bf16[2,768,2048]{2,1,0:T(8,128)(2,1)} %bitcast.98, bf16[2,2048,1536]{2,1,0:T(8,128)(2,1)} %all-gather.6.cloned.1.call-done), kind=kOutput, calls=%fused_computation.147 | convolution fusion | flops 9663676416 | bytes 28311552 | tf_op jit(solution)/shard_map/erd,edf->erf/dot_general | solution.py:186
  271.2 9.6 %convolution_convert_fusion = bf16[2,768,2048]{2,1,0:T(8,128)(2,1)S(1)} fusion(bf16[2,2048,768]{2,1,0:T(8,128)(2,1)} %all-gather.8.cloned.1.call-done, f32[2,768,1536]{2,1,0:T(8,128)} %fusion.88), kind=kOutput, calls=%fused_computation.36 | convolution fusion | flops 4842061824 | bytes 22020096 | tf_op jit(solution)/shard_map/erf,edf->erd/dot_general | solution.py:190
  292.1 10.8 %collective-permute-done = bf16[1,2,96,2048]{3,2,0,1:T(8,128)(2,1)} collective-permute-done((bf16[1,2,96,2048]{3,2,0,1:T(8,128)(2,1)}, bf16[1,2,96,2048]{3,2,0,1:T(8,128)(2,1)}, u32[]{:S(2)}, u32[]{:S(2)}) %collective-permute-start) | collective-permute-done | bytes 786464 | tf_op jit(solution)/shard_map/ppermute | solution.py:33
  305.7 15.2 %collective-permute-done.1 = bf16[1,2,96,2048]{3,2,0,1:T(8,128)(2,1)} collective-permute-done((bf16[1,2,96,2048]{3,2,0,1:T(8,128)(2,1)}, bf16[1,2,96,2048]{3,2,0,1:T(8,128)(2,1)}, u32[]{:S(2)}, u32[]{:S(2)}) %collective-permute-start.1) | collective-permute-done | bytes 786464 | tf_op jit(solution)/shard_map/ppermute | solution.py:33
  323.2 80.9 %collective-permute-done.2 = bf16[1,2,96,2048]{3,2,0,1:T(8,128)(2,1)} collective-permute-done((bf16[1,2,96,2048]{3,2,0,1:T(8,128)(2,1)}, bf16[1,2,96,2048]{3,2,0,1:T(8,128)(2,1)}, u32[]{:S(2)}, u32[]{:S(2)}) %collective-permute-start.2) | collective-permute-done | bytes 786464 | tf_op jit(solution)/shard_map/ppermute | solution.py:33
  406.2 14.7 %collective-permute-done.3 = bf16[1,2,96,2048]{3,2,0,1:T(8,128)(2,1)} collective-permute-done((bf16[1,2,96,2048]{3,2,0,1:T(8,128)(2,1)S(1)}, bf16[1,2,96,2048]{3,2,0,1:T(8,128)(2,1)}, u32[]{:S(2)}, u32[]{:S(2)}) %collective-permute-start.3) | collective-permute-done | bytes 786464 | tf_op jit(solution)/shard_map/ppermute | solution.py:33
  427.7 6.6 %copy.37 = bf16[8,2,96,2048]{3,2,1,0:T(8,128)(2,1)} copy(bf16[8,2,96,2048]{3,2,0,1:T(8,128)(2,1)} %constant_dynamic-update-slice_fusion) | data formatting | bytes 12582912 | tf_op jit(solution)/shard_map/dynamic_update_slice | solution.py:36
  434.3 10.7 %gather_fusion = bf16[768,2048]{1,0:T(8,128)(2,1)} fusion(bf16[1536,2048]{1,0:T(8,128)(2,1)} %bitcast.88, s32[1024]{0:T(1024)S(1)} %pad_clamp_fusion), kind=kCustom, calls=%fused_computation.1 | custom fusion | bytes 6294528 | tf_op jit(solution)/shard_map/gather | solution.py:192
  445.0 6.6 %reshape.292 = f32[128,6,2048]{2,1,0:T(8,128)} reshape(bf16[768,2048]{1,0:T(8,128)(2,1)} %gather_fusion) | data formatting | bytes 9437184 | tf_op jit(solution)/shard_map/convert_element_type | solution.py:193
  451.6 7.5 %multiply_reduce_fusion = bf16[128,2048]{1,0:T(8,128)(2,1)} fusion(f32[128,6,2048]{2,1,0:T(8,128)} %reshape.292, f32[128,6]{1,0:T(8,128)S(1)} %bitcast.108), kind=kLoop, calls=%fused_computation.33 | loop fusion | flops 2883584 | bytes 6818816 | tf_op jit(solution)/shard_map/reduce_sum | solution.py:194
  (115 shorter events, 62.6 us)
Async XLA Ops:
  7.2 6.0 %copy-start.11 = (s32[1,128,6]{1,0,2:T(1,128)S(1)}, s32[1,128,6]{1,0,2:T(1,128)}, u32[]{:S(2)}) copy-start(s32[1,128,6]{1,0,2:T(1,128)} %param.22) | copy-start | bytes 9220
  7.2 6.4 %copy-start.9 = (bf16[1,128,3072]{2,1,0:T(8,128)(2,1)S(1)}, bf16[1,128,3072]{2,1,0:T(8,128)(2,1)}, u32[]{:S(2)}) copy-start(bf16[1,128,3072]{2,1,0:T(8,128)(2,1)} %param.16) | copy-start | bytes 2359300
  7.2 34.5 %all-gather.4.cloned.1.call-start = ((), (), s32[]{:S(2)}) async-start(), calls=%async_computation.1 | async-start | bytes 1327104 | tf_op jit(solution)/shard_map/all_gather | solution.py:141
  12.4 241.8 %all-gather.6.cloned.1.call-start = ((), (), s32[]{:S(2)}) async-start(), calls=%async_computation.2 | async-start | bytes 15728640 | tf_op jit(solution)/shard_map/all_gather | solution.py:183
  28.0 6.0 %copy-start.12 = (bf16[2048]{0:T(1024)(128)(2,1)S(1)}, bf16[2048]{0:T(1024)(128)(2,1)}, u32[]{:S(2)}) copy-start(bf16[2048]{0:T(1024)(128)(2,1)} %param.21) | copy-start | bytes 12292
  38.2 2.0 copy-start.3
  42.0 6.2 %copy-start.6 = (bf16[1024,576]{0,1:T(8,128)(2,1)S(1)}, bf16[1024,576]{0,1:T(8,128)(2,1)}, u32[]{:S(2)}) copy-start(bf16[1024,576]{0,1:T(8,128)(2,1)} %get-tuple-element.36) | copy-start | bytes 3538948 | tf_op jit(solution)/shard_map/cond
  49.6 5.2 %copy-start.7 = (f32[1024,1024]{0,1:T(8,128)S(1)}, f32[1024,1024]{0,1:T(8,128)}, u32[]{:S(2)}) copy-start(f32[1024,1024]{0,1:T(8,128)} %get-tuple-element.41) | copy-start | bytes 12582916 | tf_op jit(solution)/shard_map/cond
  56.0 3.5 copy-start.5
  67.0 4.0 copy-start.8
  72.7 3.5 copy-start.4
  76.2 5.9 %copy-start.10 = (s32[768]{0:T(1024)S(1)}, s32[768]{0:T(1024)}, u32[]{:S(2)}) copy-start(s32[768]{0:T(1024)} %get-tuple-element.75) | copy-start | bytes 9220
  106.8 140.9 %all-to-all-start = ((bf16[16,96,2048]{2,1,0:T(8,128)(2,1)}), bf16[16,96,2048]{2,1,0:T(8,128)(2,1)}, u32[]{:S(2)}, u32[]{:S(2)}) async-start(bf16[16,96,2048]{2,1,0:T(8,128)(2,1)} %bitcast.89), calls=%async_computation | async-start | bytes 12582912 | tf_op jit(solution)/shard_map/all_to_all | solution.py:174
  112.3 158.9 %all-gather.8.cloned.1.call-start = ((), (), s32[]{:S(2)}) async-start(), calls=%async_computation.3 | async-start | bytes 7864320 | tf_op jit(solution)/shard_map/all_gather | solution.py:184
  280.7 3.4 copy-start.2
  280.7 9.5 %copy-start.13 = (f32[1,128,6]{1,0,2:T(1,128)S(1)}, f32[1,128,6]{1,0,2:T(1,128)}, u32[]{:S(2)}) copy-start(f32[1,128,6]{1,0,2:T(1,128)} %param.23) | copy-start | bytes 9220
  284.1 18.8 %collective-permute-start = (bf16[1,2,96,2048]{3,2,0,1:T(8,128)(2,1)}, bf16[1,2,96,2048]{3,2,0,1:T(8,128)(2,1)}, u32[]{:S(2)}, u32[]{:S(2)}) collective-permute-start(bf16[1,2,96,2048]{3,2,0,1:T(8,128)(2,1)} %get-tuple-element.50), channel_id=1, source_target_pairs={{0,1},{1,2},{2,3},{3,4},{4,5},{5,6},{6,7},{7,0},{8,9},{9,10},{10,1... | collective-permute-start | bytes 2359304 | tf_op jit(solution)/shard_map/ppermute | solution.py:33
  285.8 35.1 %collective-permute-start.1 = (bf16[1,2,96,2048]{3,2,0,1:T(8,128)(2,1)}, bf16[1,2,96,2048]{3,2,0,1:T(8,128)(2,1)}, u32[]{:S(2)}, u32[]{:S(2)}) collective-permute-start(bf16[1,2,96,2048]{3,2,0,1:T(8,128)(2,1)} %get-tuple-element.49), channel_id=1, source_target_pairs={{0,2},{1,3},{2,4},{3,5},{4,6},{5,7},{6,0},{7,1},{8,10},{9,11},{10,... | collective-permute-start | bytes 2359304 | tf_op jit(solution)/shard_map/ppermute | solution.py:33
  287.8 116.2 %collective-permute-start.2 = (bf16[1,2,96,2048]{3,2,0,1:T(8,128)(2,1)}, bf16[1,2,96,2048]{3,2,0,1:T(8,128)(2,1)}, u32[]{:S(2)}, u32[]{:S(2)}) collective-permute-start(bf16[1,2,96,2048]{3,2,0,1:T(8,128)(2,1)} %get-tuple-element.48), channel_id=1, source_target_pairs={{0,3},{1,4},{2,5},{3,6},{4,7},{5,0},{6,1},{7,2},{8,11},{9,12},{10,... | collective-permute-start | bytes 2359304 | tf_op jit(solution)/shard_map/ppermute | solution.py:33
  290.1 130.7 %collective-permute-start.3 = (bf16[1,2,96,2048]{3,2,0,1:T(8,128)(2,1)S(1)}, bf16[1,2,96,2048]{3,2,0,1:T(8,128)(2,1)}, u32[]{:S(2)}, u32[]{:S(2)}) collective-permute-start(bf16[1,2,96,2048]{3,2,0,1:T(8,128)(2,1)S(1)} %get-tuple-element.47), channel_id=1, source_target_pairs={{0,4},{1,5},{2,6},{3,7},{4,0},{5,1},{6,2},{7,3},{8,12},{9,13},{10,... | collective-permute-start | bytes 2359304 | tf_op jit(solution)/shard_map/ppermute | solution.py:33
  290.4 132.5 %collective-permute-start.4 = (bf16[1,2,96,2048]{3,2,0,1:T(8,128)(2,1)S(1)}, bf16[1,2,96,2048]{3,2,0,1:T(8,128)(2,1)S(1)}, u32[]{:S(2)}, u32[]{:S(2)}) collective-permute-start(bf16[1,2,96,2048]{3,2,0,1:T(8,128)(2,1)S(1)} %get-tuple-element.46), channel_id=1, source_target_pairs={{0,5},{1,6},{2,7},{3,0},{4,1},{5,2},{6,3},{7,4},{8,13},{9,14},{10,... | collective-permute-start | bytes 2359304 | tf_op jit(solution)/shard_map/ppermute | solution.py:33
  302.9 122.8 %collective-permute-start.5 = (bf16[1,2,96,2048]{3,2,0,1:T(8,128)(2,1)S(1)}, bf16[1,2,96,2048]{3,2,0,1:T(8,128)(2,1)S(1)}, u32[]{:S(2)}, u32[]{:S(2)}) collective-permute-start(bf16[1,2,96,2048]{3,2,0,1:T(8,128)(2,1)S(1)} %get-tuple-element.45), channel_id=1, source_target_pairs={{0,6},{1,7},{2,0},{3,1},{4,2},{5,3},{6,4},{7,5},{8,14},{9,15},{10,... | collective-permute-start | bytes 2359304 | tf_op jit(solution)/shard_map/ppermute | solution.py:33
  320.9 105.8 %collective-permute-start.6 = (bf16[1,2,96,2048]{3,2,0,1:T(8,128)(2,1)S(1)}, bf16[1,2,96,2048]{3,2,0,1:T(8,128)(2,1)S(1)}, u32[]{:S(2)}, u32[]{:S(2)}) collective-permute-start(bf16[1,2,96,2048]{3,2,0,1:T(8,128)(2,1)S(1)} %get-tuple-element.44), channel_id=1, source_target_pairs={{0,7},{1,0},{2,1},{3,2},{4,3},{5,4},{6,5},{7,6},{8,15},{9,8},{10,9... | collective-permute-start | bytes 2359304 | tf_op jit(solution)/shard_map/ppermute | solution.py:33
  451.6 7.5 %copy-start.1 = (bf16[2048,576]{0,1:T(8,128)(2,1)S(1)}, bf16[2048,576]{0,1:T(8,128)(2,1)}, u32[]{:S(2)}) copy-start(bf16[2048,576]{0,1:T(8,128)(2,1)} %param.17) | copy-start | bytes 7077892
  (1 other events, 1.7 us)
Sparse Core Ops, SparseCore 0:
  12.6 27.5 all-gather.3
  42.0 119.6 all-gather.5
  163.6 70.1 all-gather.7
